TPU v7x, 512 devices: a whole 4x4x16 slice. The times are simulated.
512 devices in a mesh: ctx: 64 (over y, z), tp: 8 (over x, core).
Axes of the slice: x: 4, y: 4, z: 16, core: 2. Of those that a mesh axis runs over, the one named last changes fastest.
Arguments:
- lin_query: bfloat16 [8192, 4096], P('ctx', 'tp'), may hold values from -6 to 6
- lin_key: bfloat16 [8192, 4096], P('ctx', 'tp'), may hold values from -6 to 6
- lin_value: bfloat16 [8192, 4096], P('ctx', 'tp'), may hold values from -6 to 6
- lin_cotangent: bfloat16 [8192, 4096], P('ctx', 'tp'), may hold values from -6 to 6
- soft_query: bfloat16 [8192, 4096], P('ctx', 'tp'), may hold values from -200 to 200
- soft_key: bfloat16 [8192, 1024], P('ctx', 'tp'), may hold values from -200 to 200
- soft_value: bfloat16 [8192, 1024], P('ctx', 'tp'), may hold values from -6 to 6
- doc_start: int32 [8192], P('ctx'), may hold values from 0 to 8191, as said below
Outputs:
- lin_out: bfloat16 [8192, 4096], P('ctx', 'tp')
- grad_query: bfloat16 [8192, 4096], P('ctx', 'tp')
- grad_key: bfloat16 [8192, 4096], P('ctx', 'tp')
- grad_value: bfloat16 [8192, 4096], P('ctx', 'tp')
- soft_out: bfloat16 [8192, 4096], P('ctx', 'tp')
Inputs may be any that keep to these rules, and one draw needn't show every extreme that they name: doc_start[i] <= i, doc_start never falls along the sequence, doc_start[0] = 0, doc_start[i] equals i or doc_start[i - 1], and a document of one position starts at position 8191.
All inputs are finite; a program needn't handle non-finite values.
Results may differ from a plain program's by a relative error of at most 0.011.
Values may be sent and summed in bfloat16 or wider, within the bound.
No kernel may reach another device: no remote copies, remote signals or barrier semaphores. Data moves between devices by JAX's collectives and lax.ppermute only.
A program may use at most 128 MiB of HBM per device.

v0:
```python
import math
import jax
import jax.numpy as jnp
from jax import lax
from jax.sharding import PartitionSpec as P

HD = 128
LH = 32
SH = 32
KVH = 8
epsilon = 1e-06
highest = lax.Precision.HIGHEST
floor_score = -1e30


def carried_in(value, axis, combine, identity, reverse):
    length, position = (lax.axis_size(axis), lax.axis_index(axis))
    everything = lax.all_gather(value.astype(jnp.bfloat16), axis)
    start = jnp.broadcast_to(jnp.asarray(identity, value.dtype), value.shape)

    def hop(k, before):
        at = length - 1 - k if reverse else k
        reached = at > position if reverse else at < position
        new = combine(before, everything[at].astype(value.dtype))
        return jnp.where(reached, new, before)

    return lax.fori_loop(0, length, hop, start)


def on_device(
    lin_query, lin_key, lin_value, lin_cotangent, soft_query, soft_key, soft_value, doc_start
):
    length = lin_query.shape[0]
    heads_here = lin_query.shape[1] // HD
    queries = lin_query.reshape(length, heads_here, HD)
    keys = lin_key.reshape(length, heads_here, HD)
    values = lin_value.reshape(length, heads_here, HD)
    lower = jnp.tril(jnp.ones((length, length), dtype=bool))
    raw_scores = jnp.einsum("thd,shd->hts", queries, keys, preferred_element_type=jnp.float32)
    weights = jnp.where(lower[None], raw_scores, 0.0).astype(jnp.bfloat16)
    own_state = jnp.einsum("thd,the->hde", keys, values, preferred_element_type=jnp.float32)
    earlier = carried_in(own_state, "ctx", jnp.add, jnp.zeros_like(own_state), False)
    mixed = jnp.einsum("hts,shd->thd", weights, values, preferred_element_type=jnp.float32)
    mixed = mixed + jnp.einsum(
        "thd,hde->the", queries.astype(jnp.float32), earlier, precision=highest
    )
    mixed = mixed.reshape(length, heads_here * HD)
    squares = lax.psum(jnp.sum(mixed * mixed, axis=1), "tp")
    scale = lax.rsqrt(squares / (LH * HD) + epsilon)
    normed = mixed * scale[:, None]
    lin_out = normed.astype(jnp.bfloat16)
    grad = lin_cotangent.astype(jnp.float32)
    inner = lax.psum(jnp.sum(grad * normed, axis=1), "tp")
    grad_mix = scale[:, None] * (grad - normed * (inner / (LH * HD))[:, None])
    grad_mix = grad_mix.astype(jnp.bfloat16).reshape(length, heads_here, HD)
    own_adjoint = jnp.einsum("thd,the->hde", queries, grad_mix, preferred_element_type=jnp.float32)
    later = carried_in(own_adjoint, "ctx", jnp.add, jnp.zeros_like(own_adjoint), True)
    raw_grad = jnp.einsum("the,she->hts", grad_mix, values, preferred_element_type=jnp.float32)
    grad_scores = jnp.where(lower[None], raw_grad, 0.0).astype(jnp.bfloat16)
    grad_q = jnp.einsum("hts,shd->thd", grad_scores, keys, preferred_element_type=jnp.float32)
    grad_q = grad_q + jnp.einsum(
        "the,hde->thd", grad_mix.astype(jnp.float32), earlier, precision=highest
    )
    grad_k = jnp.einsum("hts,thd->shd", grad_scores, queries, preferred_element_type=jnp.float32)
    grad_k = grad_k + jnp.einsum(
        "she,hde->shd", values.astype(jnp.float32), later, precision=highest
    )
    grad_v = jnp.einsum("hts,thd->shd", weights, grad_mix, preferred_element_type=jnp.float32)
    grad_v = grad_v + jnp.einsum("shd,hde->she", keys.astype(jnp.float32), later, precision=highest)
    grad_query = grad_q.reshape(length, heads_here * HD).astype(jnp.bfloat16)
    grad_key = grad_k.reshape(length, heads_here * HD).astype(jnp.bfloat16)
    grad_value = grad_v.reshape(length, heads_here * HD).astype(jnp.bfloat16)
    group = SH // KVH
    kv_here = soft_key.shape[1] // HD
    factor = 1.0 / math.sqrt(HD)
    soft_q = soft_query.reshape(length, kv_here, group, HD)
    my_first = lax.axis_index("ctx") * length
    query_pos = my_first + jnp.arange(length, dtype=jnp.int32)

    def attend(carry, key_rows, value_rows, start):
        count = key_rows.shape[0]
        key_pos = start + jnp.arange(count, dtype=jnp.int32)
        allowed = (key_pos[None, :] <= query_pos[:, None]) & (
            key_pos[None, :] >= doc_start[:, None]
        )
        key_heads = key_rows.reshape(count, kv_here, HD)
        value_heads = value_rows.reshape(count, kv_here, HD)
        scores = (
            jnp.einsum("tkgd,nkd->kgtn", soft_q, key_heads, preferred_element_type=jnp.float32)
            * factor
        )
        scores = jnp.where(allowed, scores, floor_score)
        old_top, old_total, old_acc = carry
        new_top = jnp.maximum(old_top, jnp.max(scores, axis=-1))
        probs = jnp.where(allowed, jnp.exp(scores - new_top[..., None]), 0.0)
        shrink = jnp.exp(old_top - new_top)
        new_total = shrink * old_total + jnp.sum(probs, axis=-1)
        update = jnp.einsum(
            "kgtn,nkd->kgtd",
            probs.astype(jnp.bfloat16),
            value_heads,
            preferred_element_type=jnp.float32,
        )
        return (new_top, new_total, shrink[..., None] * old_acc + update)

    def visit(carry, key_rows, value_rows, start):
        return attend(carry, key_rows, value_rows, start)

    initial = (
        jnp.full((kv_here, group, length), floor_score, jnp.float32),
        jnp.zeros((kv_here, group, length), jnp.float32),
        jnp.zeros((kv_here, group, length, HD), jnp.float32),
    )
    key_rows = lax.all_gather(soft_key, "ctx", axis=0, tiled=True)
    value_rows = lax.all_gather(soft_value, "ctx", axis=0, tiled=True)
    count = key_rows.shape[0]
    block = math.gcd(count, 512)

    def inner_step(index, state):
        key_part = lax.dynamic_slice_in_dim(key_rows, index * block, block, 0)
        value_part = lax.dynamic_slice_in_dim(value_rows, index * block, block, 0)
        return visit(state, key_part, value_part, index * block)

    final = lax.fori_loop(0, count // block, inner_step, initial)
    top, total, accum = final
    result = accum / total[..., None]
    soft_out = (
        jnp.transpose(result, (2, 0, 1, 3))
        .reshape(length, kv_here * group * HD)
        .astype(jnp.bfloat16)
    )
    return (lin_out, grad_query, grad_key, grad_value, soft_out)


def solution(mesh):
    placed = (
        P("ctx", "tp"),
        P("ctx", "tp"),
        P("ctx", "tp"),
        P("ctx", "tp"),
        P("ctx", "tp"),
        P("ctx", "tp"),
        P("ctx", "tp"),
        P("ctx"),
    )
    return jax.shard_map(
        on_device,
        mesh=mesh,
        in_specs=placed,
        out_specs=(P("ctx", "tp"), P("ctx", "tp"), P("ctx", "tp"), P("ctx", "tp"), P("ctx", "tp")),
        check_vma=False,
    )
```

profile of v0, /device:TPU:2, one launch (start us, length us, event | category | flops | bytes accessed | tf_op | source)
XLA Modules:
  0.0 685.3 jit_solution(14521103591499810169)
XLA Ops:
  8.3 1.7 convolution_convert_fusion.1
  15.1 157.9 %all-gather.11.cloned.1.call-done = bf16[256,128,128]{2,1,0:T(8,128)(2,1)} async-done(((bf16[4,128,128]{2,1,0:T(8,128)(2,1)}), bf16[256,128,128]{2,1,0:T(8,128)(2,1)}) %all-gather.11.cloned.1.call-update) | async-done | bytes 8388624 | tf_op jit(solution)/shard_map/all_gather | solution.py:18
  173.0 67.9 %while.48 = (s32[]{:T(128)}, f32[4,128,128]{2,1,0:T(8,128)S(1)}, s32[]{:T(128)}, bf16[64,4,128,128]{3,2,1,0:T(8,128)(2,1)}, s32[]{:T(128)}, /*index=5*/s32[]{:T(128)}) while((s32[]{:T(128)}, f32[4,128,128]{2,1,0:T(8,128)S(1)}, s32[]{:T(128)}, bf16[64,4,128,128]{3,2,1,0:T(8,128)(2,1)}, s32[]{:T(128)}, /*index=5*/s32[]{:T(128)}) %tuple.131), condition=%wide.region_1.2_spmd.clone, body=%wide.region_0.1_spmd.clone.sunk | while | flops 262148 | bytes 655453 | solution.py:27
  241.5 10.0 %psum.14 = f32[128]{0:T(128)S(1)} all-reduce(f32[128]{0:T(128)S(1)} %get-tuple-element.497), channel_id=1, replica_groups=mesh['ctx'=64,'tp'=8] {'tp'}, use_global_device_ids=true, to_apply=%region_3.4 | all-reduce | flops 128 | bytes 1024 | tf_op jit(solution)/shard_map/psum | solution.py:48
  251.7 13.2 %psum.15 = f32[128]{0:T(128)S(1)} all-reduce(f32[128]{0:T(128)S(1)} %fusion.30), channel_id=1, replica_groups=mesh['ctx'=64,'tp'=8] {'tp'}, use_global_device_ids=true, to_apply=%region_5.6 | all-reduce | flops 128 | bytes 1024 | tf_op jit(solution)/shard_map/psum | solution.py:53
  266.8 45.0 %all-gather.7.cloned.1.call-done = bf16[8192,128]{1,0:T(8,128)(2,1)} async-done(((bf16[128,128]{1,0:T(8,128)(2,1)}), bf16[8192,128]{1,0:T(8,128)(2,1)}) %all-gather.7.cloned.1.call-update) | async-done | bytes 2097168 | tf_op jit(solution)/shard_map/all_gather | solution.py:114
  311.8 139.9 %all-gather.9.cloned.1.call-done = bf16[8192,128]{1,0:T(8,128)(2,1)} async-done(((bf16[128,128]{1,0:T(8,128)(2,1)}), bf16[8192,128]{1,0:T(8,128)(2,1)}) %all-gather.9.cloned.1.call-update) | async-done | bytes 2097168 | tf_op jit(solution)/shard_map/all_gather | solution.py:115
  451.7 48.5 %while.50 = (s32[]{:T(128)}, f32[1,4,128]{2,1,0:T(4,128)S(1)}, f32[1,4,128]{2,1,0:T(4,128)S(1)}, f32[1,4,128,128]{3,2,1,0:T(8,128)S(1)}, s32[128]{0:T(128)S(1)},...) while((s32[]{:T(128)}, f32[1,4,128]{2,1,0:T(4,128)S(1)}, ...), condition=%wide.region_11.12_spmd.clone, body=%wide.region_8.11_spmd.clone.sunk | while | flops 136973952 | bytes 4363975 | solution.py:124
  453.1 1.4 fusion.91
  454.9 1.2 fusion.88
  456.1 1.4 fusion.91
  459.2 1.4 fusion.91
  461.0 1.2 fusion.88
  462.2 1.4 fusion.91
  465.2 1.4 fusion.91
  467.0 1.2 fusion.88
  468.3 1.4 fusion.91
  471.3 1.4 fusion.91
  474.3 1.4 fusion.91
  477.4 1.4 fusion.91
  480.4 1.4 fusion.91
  483.4 1.4 fusion.91
  485.2 1.2 fusion.88
  486.5 1.4 fusion.91
  489.5 1.4 fusion.91
  491.3 1.2 fusion.88
  492.5 1.4 fusion.91
  495.6 1.4 fusion.91
  497.3 1.2 fusion.88
  498.6 1.4 fusion.91
  503.1 105.1 %all-gather.13.cloned.1.call-done = bf16[256,128,128]{2,1,0:T(8,128)(2,1)} async-done(((bf16[4,128,128]{2,1,0:T(8,128)(2,1)}), bf16[256,128,128]{2,1,0:T(8,128)(2,1)}) %all-gather.13.cloned.1.call-update) | async-done | bytes 8388624 | tf_op jit(solution)/shard_map/all_gather | solution.py:18
  608.1 68.2 %while.49 = (s32[]{:T(128)}, f32[4,128,128]{2,1,0:T(8,128)S(1)}, s32[]{:T(128)}, bf16[64,4,128,128]{3,2,1,0:T(8,128)(2,1)}, s32[]{:T(128)}, /*index=5*/s32[]{:T(128)}, s32[]{:T(128)}, s32[]{:T(128)}) while((s32[]{:T(128)}, f32[4,128,128]{2,1,0:T(8,128)S(1)}, s32[]{:T(128)}, bf16[64,4,128,128]{3,2,1,0:T(8,128)(2,1)}, s32[]{:T(128)}, ...), condition=%wide.region_7.8_spmd.clone, body=%wide.region_6.7_spmd.clone.sunk | while | flops 262152 | bytes 655515 | solution.py:27
  (301 shorter events, 165.0 us)
Async XLA Ops:
  7.2 4.5 copy-start
  7.2 165.8 %all-gather.11.cloned.1.call-start = ((), (), s32[]{:S(2)}) async-start(), calls=%async_computation.2 | async-start | bytes 8519680 | tf_op jit(solution)/shard_map/all_gather | solution.py:18
  10.0 301.8 %all-gather.7.cloned.1.call-start = ((), (), s32[]{:S(2)}) async-start(), calls=%async_computation | async-start | bytes 2129920 | tf_op jit(solution)/shard_map/all_gather | solution.py:114
  10.8 440.9 %all-gather.9.cloned.1.call-start = ((), (), s32[]{:S(2)}) async-start(), calls=%async_computation.1 | async-start | bytes 2129920 | tf_op jit(solution)/shard_map/all_gather | solution.py:115
  11.5 596.6 %all-gather.13.cloned.1.call-start = ((), (), s32[]{:S(2)}) async-start(), calls=%async_computation.3 | async-start | bytes 8519680 | tf_op jit(solution)/shard_map/all_gather | solution.py:18
  173.0 78.5 %copy-start.2 = (bf16[128,512]{1,0:T(8,128)(2,1)S(1)}, bf16[128,512]{1,0:T(8,128)(2,1)}, u32[]{:S(2)}) copy-start(bf16[128,512]{1,0:T(8,128)(2,1)} %param.17) | copy-start | bytes 393220
  240.9 210.8 %copy-start.4 = (s32[128]{0:T(128)S(1)}, s32[128]{0:T(128)}, u32[]{:S(2)}) copy-start(s32[128]{0:T(128)} %param.21) | copy-start | bytes 1540
  451.7 49.4 %copy-start.1 = (bf16[128,512]{1,0:T(8,128)(2,1)S(1)}, bf16[128,512]{1,0:T(8,128)(2,1)}, u32[]{:S(2)}) copy-start(bf16[128,512]{1,0:T(8,128)(2,1)} %param.16) | copy-start | bytes 393220
  502.8 173.6 %copy-start.3 = (bf16[128,512]{1,0:T(8,128)(2,1)S(1)}, bf16[128,512]{1,0:T(8,128)(2,1)}, u32[]{:S(2)}) copy-start(bf16[128,512]{1,0:T(8,128)(2,1)} %param.15) | copy-start | bytes 393220
Sparse Core Ops, SparseCore 0:
  11.5 161.4 all-gather.10
  176.0 135.8 all-gather.6
  314.8 136.8 all-gather.8
  455.1 153.0 all-gather.12
where the time goes:
time: 688 us; the launch traced here: 685 us
  waiting for transfers between devices  449 us (65%)
  other arithmetic  140 us (20%)
  matrix products  47.7 us (7%)
  blocking collectives  23.2 us (3%)
  between operations  14 us (2%)
    all_gather x2, waiting for transfers between devices, carried_in(): everything = lax.all_gather(value.astype(jnp.bfloat16), axis)  263 us
    all_gather x1, waiting for transfers between devices, on_device(): value_rows = lax.all_gather(soft_value, 'ctx', axis=0, tiled=True)  140 us
    select_n x128, other arithmetic, hop(): return jnp.where(reached, new, before)  133 us
    all_gather x1, waiting for transfers between devices, on_device(): key_rows = lax.all_gather(soft_key, 'ctx', axis=0, tiled=True)  45 us
    dot_general x16, matrix products, attend(): jnp.einsum('kgtn,nkd->kgtd', probs.astype(jnp.bfloat16), value_heads, pre...  21.7 us
    dot_general x16, matrix products, attend(): jnp.einsum('tkgd,nkd->kgtn', soft_q, key_heads, preferred_element_type=jn...  19.5 us
  transfers between devices with their start and end apart: 4, of which 4 were waited for; matrix products, arithmetic and copies ran while one was open for 18% of the time, Pallas kernels for 0%

commit v1 on v0

--- a/solution.py
+++ b/solution.py
@@ -112,7 +112,9 @@
         jnp.zeros((kv_here, group, length, HD), jnp.float32),
     )
     key_rows = lax.all_gather(soft_key, "ctx", axis=0, tiled=True)
-    value_rows = lax.all_gather(soft_value, "ctx", axis=0, tiled=True)
+    value_rows = jnp.concatenate(
+        lax.all_to_all(jnp.stack([soft_value] * lax.axis_size("ctx")), "ctx", 0, 0), axis=0
+    )
     count = key_rows.shape[0]
     block = math.gcd(count, 512)
 

time: 688 us -> 577 us (0.84)
  waiting for transfers between devices: 449 us -> 319 us
  starting transfers between devices: 0.16 us -> 19.2 us
    all_gather x1 -> x0, waiting for transfers between devices: 140 us -> none  [on_device(): value_rows = lax.all_gather(soft_value, 'ctx', axis=0, tiled=True)]
    all_to_all x0 -> x1, starting transfers between devices: none -> 19.1 us  [on_device(): lax.all_to_all(jnp.stack([soft_value] * lax.axis_size('ctx')), 'ctx', 0, 0)]
    all_gather x2, waiting for transfers between devices: 263 us -> 274 us  [carried_in(): everything = lax.all_gather(value.astype(jnp.bfloat16), axis)]
  transfers between devices with their start and end apart: 4 -> 4, of which waited for: 4 -> 3; matrix products, arithmetic and copies ran while one was open for 18% -> 21% of each run, Pallas kernels for 0% -> 0%
where the time goes in v1:
time: 577 us; the launch traced here: 574 us
  waiting for transfers between devices  319 us (55%)
  other arithmetic  140 us (24%)
  matrix products  45.9 us (8%)
  blocking collectives  23.3 us (4%)
  starting transfers between devices  19.2 us (3%)
  between operations  14 us (2%)
  local copies, waits for them, and re-layouts  8.09 us (1%)
    all_gather x2, waiting for transfers between devices, carried_in(): everything = lax.all_gather(value.astype(jnp.bfloat16), axis)  274 us
    select_n x128, other arithmetic, hop(): return jnp.where(reached, new, before)  133 us
    all_gather x1, waiting for transfers between devices, on_device(): key_rows = lax.all_gather(soft_key, 'ctx', axis=0, tiled=True)  44.5 us
    dot_general x16, matrix products, attend(): jnp.einsum('kgtn,nkd->kgtd', probs.astype(jnp.bfloat16), value_heads, pre...  21.7 us
    dot_general x16, matrix products, attend(): jnp.einsum('tkgd,nkd->kgtn', soft_q, key_heads, preferred_element_type=jn...  19.6 us
    all_to_all x1, starting transfers between devices, on_device(): lax.all_to_all(jnp.stack([soft_value] * lax.axis_size('ctx')), 'ctx', 0, 0)  19.1 us
    psum x1, blocking collectives, on_device(): inner = lax.psum(jnp.sum(grad * normed, axis=1), 'tp')  13.3 us
  transfers between devices with their start and end apart: 4, of which 3 were waited for; matrix products, arithmetic and copies ran while one was open for 21% of the time, Pallas kernels for 0%

profile of v1, /device:TPU:2, one launch (start us, length us, event | category | flops | bytes accessed | tf_op | source)
XLA Modules:
  0.0 573.8 jit_solution(14497119870010064305)
XLA Ops:
  8.3 1.7 convolution_convert_fusion.1
  10.0 2.6 stack.2
  12.7 19.1 %all-to-all-start = ((bf16[64,128,128]{2,1,0:T(8,128)(2,1)}), bf16[64,128,128]{2,1,0:T(8,128)(2,1)}, u32[]{:S(2)}, u32[]{:S(2)}) async-start(bf16[64,128,128]{2,1,0:T(8,128)(2,1)} %stack.2), calls=%async_computation | async-start | bytes 4194304 | tf_op jit(solution)/shard_map/all_to_all | solution.py:116
  33.4 168.2 %all-gather.8.cloned.1.call-done = bf16[256,128,128]{2,1,0:T(8,128)(2,1)} async-done(((bf16[4,128,128]{2,1,0:T(8,128)(2,1)}), bf16[256,128,128]{2,1,0:T(8,128)(2,1)}) %all-gather.8.cloned.1.call-update) | async-done | bytes 8388624 | tf_op jit(solution)/shard_map/all_gather | solution.py:18
  201.6 67.9 %while.48 = (s32[]{:T(128)}, f32[4,128,128]{2,1,0:T(8,128)S(1)}, s32[]{:T(128)}, bf16[64,4,128,128]{3,2,1,0:T(8,128)(2,1)}, s32[]{:T(128)}, /*index=5*/s32[]{:T(128)}) while((s32[]{:T(128)}, f32[4,128,128]{2,1,0:T(8,128)S(1)}, s32[]{:T(128)}, bf16[64,4,128,128]{3,2,1,0:T(8,128)(2,1)}, s32[]{:T(128)}, /*index=5*/s32[]{:T(128)}) %tuple.129), condition=%wide.region_1.2_spmd.clone, body=%wide.region_0.1_spmd.clone.sunk | while | flops 262148 | bytes 655453 | solution.py:27
  270.1 10.0 %psum.14 = f32[128]{0:T(128)S(1)} all-reduce(f32[128]{0:T(128)S(1)} %get-tuple-element.497), channel_id=1, replica_groups=mesh['ctx'=64,'tp'=8] {'tp'}, use_global_device_ids=true, to_apply=%region_3.4 | all-reduce | flops 128 | bytes 1024 | tf_op jit(solution)/shard_map/psum | solution.py:48
  280.3 13.3 %psum.15 = f32[128]{0:T(128)S(1)} all-reduce(f32[128]{0:T(128)S(1)} %fusion.30), channel_id=1, replica_groups=mesh['ctx'=64,'tp'=8] {'tp'}, use_global_device_ids=true, to_apply=%region_5.6 | all-reduce | flops 128 | bytes 1024 | tf_op jit(solution)/shard_map/psum | solution.py:53
  295.5 44.5 %all-gather.6.cloned.1.call-done = bf16[8192,128]{1,0:T(8,128)(2,1)} async-done(((bf16[128,128]{1,0:T(8,128)(2,1)}), bf16[8192,128]{1,0:T(8,128)(2,1)}) %all-gather.6.cloned.1.call-update) | async-done | bytes 2097168 | tf_op jit(solution)/shard_map/all_gather | solution.py:114
  339.9 48.5 %while.50 = (s32[]{:T(128)}, f32[1,4,128]{2,1,0:T(4,128)S(1)}, f32[1,4,128]{2,1,0:T(4,128)S(1)}, f32[1,4,128,128]{3,2,1,0:T(8,128)S(1)}, s32[128]{0:T(128)S(1)},...) while((s32[]{:T(128)}, f32[1,4,128]{2,1,0:T(4,128)S(1)}, ...), condition=%wide.region_11.12_spmd.clone, body=%wide.region_8.11_spmd.clone.sunk | while | flops 136973952 | bytes 4363975 | solution.py:126
  341.3 1.4 fusion.91
  344.4 1.4 fusion.91
  347.4 1.4 fusion.91
  349.2 1.2 fusion.88
  350.4 1.4 fusion.91
  353.5 1.4 fusion.91
  355.3 1.2 fusion.88
  356.5 1.4 fusion.91
  359.5 1.4 fusion.91
  361.3 1.2 fusion.88
  362.6 1.4 fusion.91
  365.6 1.4 fusion.91
  368.6 1.4 fusion.91
  370.4 1.2 fusion.88
  371.7 1.4 fusion.91
  374.7 1.4 fusion.91
  377.7 1.4 fusion.91
  380.8 1.4 fusion.91
  383.8 1.4 fusion.91
  385.6 1.2 fusion.88
  386.8 1.4 fusion.91
  391.3 105.5 %all-gather.10.cloned.1.call-done = bf16[256,128,128]{2,1,0:T(8,128)(2,1)} async-done(((bf16[4,128,128]{2,1,0:T(8,128)(2,1)}), bf16[256,128,128]{2,1,0:T(8,128)(2,1)}) %all-gather.10.cloned.1.call-update) | async-done | bytes 8388624 | tf_op jit(solution)/shard_map/all_gather | solution.py:18
  496.8 68.2 %while.49 = (s32[]{:T(128)}, f32[4,128,128]{2,1,0:T(8,128)S(1)}, s32[]{:T(128)}, bf16[64,4,128,128]{3,2,1,0:T(8,128)(2,1)}, s32[]{:T(128)}, /*index=5*/s32[]{:T(128)}, s32[]{:T(128)}, s32[]{:T(128)}) while((s32[]{:T(128)}, f32[4,128,128]{2,1,0:T(8,128)S(1)}, s32[]{:T(128)}, bf16[64,4,128,128]{3,2,1,0:T(8,128)(2,1)}, s32[]{:T(128)}, ...), condition=%wide.region_7.8_spmd.clone, body=%wide.region_6.7_spmd.clone.sunk | while | flops 262152 | bytes 655515 | solution.py:27
  (303 shorter events, 162.7 us)
Async XLA Ops:
  7.2 25.5 %copy-start = (bf16[128,512]{1,0:T(8,128)(2,1)S(1)}, bf16[128,512]{1,0:T(8,128)(2,1)}, u32[]{:S(2)}) copy-start(bf16[128,512]{1,0:T(8,128)(2,1)} %param.14) | copy-start | bytes 393220
  7.2 194.4 %all-gather.8.cloned.1.call-start = ((), (), s32[]{:S(2)}) async-start(), calls=%async_computation.2 | async-start | bytes 8519680 | tf_op jit(solution)/shard_map/all_gather | solution.py:18
  12.6 20.0 %copy-start.3 = (bf16[128,512]{1,0:T(8,128)(2,1)S(1)}, bf16[128,512]{1,0:T(8,128)(2,1)}, u32[]{:S(2)}) copy-start(bf16[128,512]{1,0:T(8,128)(2,1)} %param.15) | copy-start | bytes 393220
  12.6 20.3 %copy-start.1 = (bf16[128,512]{1,0:T(8,128)(2,1)S(1)}, bf16[128,512]{1,0:T(8,128)(2,1)}, u32[]{:S(2)}) copy-start(bf16[128,512]{1,0:T(8,128)(2,1)} %param.16) | copy-start | bytes 393220
  12.6 20.5 %copy-start.4 = (bf16[128,512]{1,0:T(8,128)(2,1)S(1)}, bf16[128,512]{1,0:T(8,128)(2,1)}, u32[]{:S(2)}) copy-start(bf16[128,512]{1,0:T(8,128)(2,1)} %param.18) | copy-start | bytes 393220
  12.7 327.3 %all-to-all-start = ((bf16[64,128,128]{2,1,0:T(8,128)(2,1)}), bf16[64,128,128]{2,1,0:T(8,128)(2,1)}, u32[]{:S(2)}, u32[]{:S(2)}) async-start(bf16[64,128,128]{2,1,0:T(8,128)(2,1)} %stack.2), calls=%async_computation | async-start | bytes 4194304 | tf_op jit(solution)/shard_map/all_to_all | solution.py:116
  31.8 308.1 %all-gather.6.cloned.1.call-start = ((), (), s32[]{:S(2)}) async-start(), calls=%async_computation.1 | async-start | bytes 2129920 | tf_op jit(solution)/shard_map/all_gather | solution.py:114
  32.5 464.2 %all-gather.10.cloned.1.call-start = ((), (), s32[]{:S(2)}) async-start(), calls=%async_computation.3 | async-start | bytes 8519680 | tf_op jit(solution)/shard_map/all_gather | solution.py:18
  201.6 78.5 %copy-start.2 = (bf16[128,512]{1,0:T(8,128)(2,1)S(1)}, bf16[128,512]{1,0:T(8,128)(2,1)}, u32[]{:S(2)}) copy-start(bf16[128,512]{1,0:T(8,128)(2,1)} %param.17) | copy-start | bytes 393220
  269.5 70.5 %copy-start.5 = (s32[128]{0:T(128)S(1)}, s32[128]{0:T(128)}, u32[]{:S(2)}) copy-start(s32[128]{0:T(128)} %param.21) | copy-start | bytes 1540
Sparse Core Ops, SparseCore 0:
  11.5 190.0 all-gather.7
  204.6 135.3 all-gather.5
  343.5 153.2 all-gather.9
